TPU v7x, 32 devices: a whole 2x2x4 slice. The times are simulated.
32 devices in a mesh: seq: 16 (over z, y, core), mp: 2 (over x).
Axes of the slice: x: 2, y: 2, z: 4, core: 2. Of those that a mesh axis runs over, the one named last changes fastest.
Arguments:
- tokens: bfloat16 [2048, 3584], P('seq'), may hold values from -6 to 6
- query_weight: bfloat16 [3584, 4096], P('seq', 'mp'), may hold values from -0.09375 to 0.09375
- key_weight: bfloat16 [3584, 4096], P('seq', 'mp'), may hold values from -0.09375 to 0.09375
- value_weight: bfloat16 [3584, 4096], P('seq', 'mp'), may hold values from -0.09375 to 0.09375
- adapter_down_maps: bfloat16 [3584, 128], replicated, may hold values from -0.09375 to 0.09375
- lifting_matrices: bfloat16 [2, 64, 4096], P(None, None, 'mp'), may hold values from -0.75 to 0.75
- decay_logarithms: float32 [32, 2048], P('mp', 'seq'), may hold values from -1 to 0, as said below
- output_gradient: bfloat16 [2048, 4096], P('seq', 'mp'), may hold values from -0.13183594 to 0.13183594
Outputs:
- grad_down: float32 [3584, 128], P(('seq', 'mp'))
- grad_up: float32 [2, 64, 4096], P(None, None, 'mp')
Inputs may be any that keep to these rules, and one draw needn't show every extreme that they name: `decay_logarithms`: every entry is negative.
All inputs are finite; a program needn't handle non-finite values.
Results may differ from a plain program's by a relative error of at most 0.006.
Values may be sent and summed in bfloat16 or wider, within the bound.
A program may use at most 192 MiB of HBM per device.

v0:
```python
import jax
import jax.numpy as jnp
from jax import lax
from jax.sharding import PartitionSpec as P

adapter_scale = 2.0
eps_norm = 1e-06
exact_arithmetic = lax.Precision.HIGHEST


def carried_in(value, axis, join, neutral, backward):
    count, mine = (lax.axis_size(axis), lax.axis_index(axis))
    pieces = jax.tree.map(lambda part: lax.all_gather(part, axis), value)
    if backward:
        pieces = jax.tree.map(lambda part: part[::-1], pieces)
        mine = count - 1 - mine
    so_far = jax.tree.map(
        lambda part, zero: jnp.full_like(part, 0) + jnp.asarray(zero, part.dtype), value, neutral
    )

    def hop(position, so_far):
        longer = join(so_far, jax.tree.map(lambda part: part[position], pieces))
        return jax.tree.map(lambda new, old: jnp.where(position < mine, new, old), longer, so_far)

    return lax.fori_loop(0, count - 1, hop, so_far)


def combine(earlier, later):
    return (earlier[0] * later[0], later[0][:, None, None] * earlier[1] + later[1])


def split_heads(flat, heads):
    return flat.reshape(flat.shape[0], heads, flat.shape[1] // heads).transpose(1, 0, 2)


def join_heads(arr):
    return arr.transpose(1, 0, 2).reshape(arr.shape[1], arr.shape[0] * arr.shape[2])


def on_device(
    tokens,
    query_weight,
    key_weight,
    value_weight,
    adapter_down_maps,
    lifting_matrices,
    decay_logarithms,
    output_gradient,
):
    length = tokens.shape[0]
    heads = decay_logarithms.shape[0]
    rank_index = lifting_matrices.shape[1]
    low_product = jnp.dot(tokens, adapter_down_maps, preferred_element_type=jnp.float32).astype(
        jnp.bfloat16
    )
    query_low_product = low_product[:, :rank_index]
    value_low_product = low_product[:, rank_index:]
    cumulative = jnp.cumsum(decay_logarithms, axis=1)
    total = cumulative[:, -1]
    gain = jnp.exp(total)
    tail = jnp.exp(total[:, None] - cumulative)
    lead = jnp.exp(cumulative)
    causal = jnp.arange(length)[:, None] >= jnp.arange(length)[None, :]
    spread = cumulative[:, :, None] - cumulative[:, None, :]
    decay_mat = jnp.where(causal[None], jnp.exp(jnp.where(causal[None], spread, 0.0)), 0.0)
    pieces = (
        lax.all_gather(query_weight, "seq", axis=0, tiled=True),
        lax.all_gather(key_weight, "seq", axis=0, tiled=True),
        lax.all_gather(value_weight, "seq", axis=0, tiled=True),
    )
    columns = tokens
    query_frozen_part, key_base, value_frozen_part = tuple(
        (jnp.dot(columns, piece, preferred_element_type=jnp.float32) for piece in pieces)
    )
    value_before_norm = value_frozen_part + adapter_scale * jnp.dot(
        value_low_product, lifting_matrices[1], preferred_element_type=jnp.float32
    )
    key_heads = split_heads(jax.nn.silu(key_base).astype(jnp.bfloat16), heads)
    value_heads = split_heads(value_before_norm.astype(jnp.bfloat16), heads)
    key_f = key_heads.astype(jnp.float32)
    local = jnp.einsum(
        "hsi,hsj->hij",
        key_f * tail[:, :, None],
        value_heads.astype(jnp.float32),
        precision=exact_arithmetic,
    )
    state_in = carried_in(
        (gain, local), "seq", combine, (jnp.ones_like(gain), jnp.zeros_like(local)), False
    )[1]
    key_heads, key_f, value_heads, state_in = (key_heads, key_f, value_heads, state_in)
    query_before_norm = query_frozen_part + adapter_scale * jnp.dot(
        query_low_product, lifting_matrices[0], preferred_element_type=jnp.float32
    )
    query_heads = split_heads(jax.nn.silu(query_before_norm).astype(jnp.bfloat16), heads)
    query_f = query_heads.astype(jnp.float32)
    scores = jnp.einsum("htd,hsd->hts", query_heads, key_heads, preferred_element_type=jnp.float32)
    mixed = (scores * decay_mat).astype(jnp.bfloat16)
    attn = jnp.einsum(
        "hts,hsj->htj", mixed, value_heads, preferred_element_type=jnp.float32
    ) + lead[:, :, None] * jnp.einsum("hti,hij->htj", query_f, state_in, precision=exact_arithmetic)
    rms = jnp.sqrt(jnp.mean(attn * attn, axis=-1, keepdims=True) + eps_norm)
    normed = attn / rms
    upstream = split_heads(output_gradient, heads).astype(jnp.float32)
    d_attn = (upstream - normed * jnp.mean(upstream * normed, axis=-1, keepdims=True)) / rms
    d_attn_b = d_attn.astype(jnp.bfloat16)
    carried = jnp.einsum(
        "hti,htj->hij", query_f * lead[:, :, None], d_attn, precision=exact_arithmetic
    )
    later = carried_in(
        (gain, carried), "seq", combine, (jnp.ones_like(gain), jnp.zeros_like(carried)), True
    )[1]
    d_mixed = (
        jnp.einsum("htj,hsj->hts", d_attn_b, value_heads, preferred_element_type=jnp.float32)
        * decay_mat
    ).astype(jnp.bfloat16)
    d_query = jnp.einsum(
        "hts,hsi->hti", d_mixed, key_heads, preferred_element_type=jnp.float32
    ) + lead[:, :, None] * jnp.einsum("htj,hij->hti", d_attn, state_in, precision=exact_arithmetic)
    d_value = jnp.einsum(
        "hts,htj->hsj", mixed, d_attn_b, preferred_element_type=jnp.float32
    ) + tail[:, :, None] * jnp.einsum("hsi,hij->hsj", key_f, later, precision=exact_arithmetic)
    sig = jax.nn.sigmoid(query_before_norm)
    query_pre_gradient = join_heads(d_query) * (sig * (1.0 + query_before_norm * (1.0 - sig)))
    value_flat_gradient = join_heads(d_value)
    low_product_float = low_product.astype(jnp.float32)
    up_products = jnp.stack(
        [
            adapter_scale
            * jnp.dot(
                low_product_float[:, :rank_index].T, query_pre_gradient, precision=exact_arithmetic
            ),
            adapter_scale
            * jnp.dot(
                low_product_float[:, rank_index:].T, value_flat_gradient, precision=exact_arithmetic
            ),
        ]
    )
    grad_up = lax.psum(up_products, "seq")
    low_gradient = adapter_scale * jnp.concatenate(
        [
            jnp.dot(
                query_pre_gradient,
                lifting_matrices[0].astype(jnp.float32).T,
                precision=exact_arithmetic,
            ),
            jnp.dot(
                value_flat_gradient,
                lifting_matrices[1].astype(jnp.float32).T,
                precision=exact_arithmetic,
            ),
        ],
        axis=1,
    )
    seq_count = lax.axis_size("seq")
    model_count = lax.axis_size("mp")
    own_rows = tokens.shape[1] // (seq_count * model_count)
    whole_low = lax.psum(low_gradient, "mp")
    grouped = tokens.reshape(length, seq_count, model_count, own_rows)
    mine = lax.dynamic_index_in_dim(grouped, lax.axis_index("mp"), 2, keepdims=False).reshape(
        length, seq_count * own_rows
    )
    columns = mine.astype(jnp.float32)
    grad_down = lax.psum_scatter(
        jnp.dot(columns.T, whole_low, precision=exact_arithmetic),
        "seq",
        scatter_dimension=0,
        tiled=True,
    )
    return (grad_down, grad_up)


def solution(mesh):
    return jax.shard_map(
        on_device,
        mesh=mesh,
        in_specs=(
            P("seq", None),
            P("seq", "mp"),
            P("seq", "mp"),
            P("seq", "mp"),
            P(),
            P(None, None, "mp"),
            P("mp", "seq"),
            P("seq", "mp"),
        ),
        out_specs=(P(("seq", "mp"), None), P(None, None, "mp")),
        check_vma=False,
    )
```

profile of v0, /device:TPU:0, one launch (start us, length us, event | category | flops | bytes accessed | tf_op | source)
XLA Modules:
  0.0 865.7 jit_solution(1407161267636139676)
XLA Ops:
  11.7 1.7 convolution_convert_fusion
  13.3 113.6 %all-gather.13.cloned.1.call-done = bf16[3584,2048]{1,0:T(8,128)(2,1)} async-done(((bf16[224,2048]{1,0:T(8,128)(2,1)}), bf16[3584,2048]{1,0:T(8,128)(2,1)}) %all-gather.13.cloned.1.call-update) | async-done | bytes 14680080 | tf_op jit(solution)/shard_map/all_gather | solution.py:69
  126.9 7.5 fusion.54
  134.8 106.4 %all-gather.11.cloned.1.call-done = bf16[3584,2048]{1,0:T(8,128)(2,1)} async-done(((bf16[224,2048]{1,0:T(8,128)(2,1)}), bf16[3584,2048]{1,0:T(8,128)(2,1)}) %all-gather.11.cloned.1.call-update) | async-done | bytes 14680080 | tf_op jit(solution)/shard_map/all_gather | solution.py:68
  241.3 7.3 multiply_convert_fusion
  248.6 2.3 fusion.17
  252.6 32.0 %all-reduce = f32[256]{0:T(256)S(1)} all-reduce(f32[256]{0:T(256)S(1)} %dynamic-update-slice), channel_id=2, replica_groups=mesh['seq'=16,'mp'=2] {'seq'}, use_global_device_ids=true, to_apply=%add | all-reduce | flops 256 | bytes 2048
  284.7 2.2 copy.40
  286.9 69.0 %all-gather.9.cloned.1.call-done = bf16[3584,2048]{1,0:T(8,128)(2,1)} async-done(((bf16[224,2048]{1,0:T(8,128)(2,1)}), bf16[3584,2048]{1,0:T(8,128)(2,1)}) %all-gather.9.cloned.1.call-update) | async-done | bytes 14680080 | tf_op jit(solution)/shard_map/all_gather | solution.py:67
  356.0 7.2 fusion.53
  363.2 2.7 multiply_convert_fusion.1
  369.9 1.5 fusion.21
  371.4 112.3 %all-gather.15.cloned.1.call-done = f32[256,128,128]{2,1,0:T(8,128)} async-done(((f32[16,128,128]{2,1,0:T(8,128)}), f32[256,128,128]{2,1,0:T(8,128)}) %all-gather.15.cloned.1.call-update) | async-done | bytes 16777232 | tf_op jit(solution)/shard_map/all_gather | solution.py:13
  483.7 22.5 %while.28 = (s32[]{:T(128)}, f32[16,128,128]{2,1,0:T(8,128)S(1)}, s32[]{:T(128)}, f32[16,16]{1,0:T(8,128)S(1)}, f32[16,16,128,128]{3,2,1,0:T(8,128)}, /*index=5*/s32[]{:T(128)}, s32[]{:T(128)}) while((s32[]{:T(128)}, f32[16,128,128]{2,1,0:T(8,128)S(1)}, s32[]{:T(128)}, f32[16,16]{1,0:T(8,128)S(1)}, f32[16,16,128,128]{3,2,1,0:T(8,128)}, ...), condition=%wide.region_2.3_spmd.clone, body=%wide.region_1.2_spmd.clone.sunk | while | flops 1048580 | bytes 3146025 | solution.py:25
  483.7 1.5 fusion.86
  485.2 1.5 fusion.86
  488.2 1.5 fusion.86
  489.7 1.5 fusion.86
  492.7 1.5 fusion.86
  494.2 1.5 fusion.86
  495.7 1.5 fusion.86
  497.2 1.5 fusion.86
  500.2 1.5 fusion.86
  501.7 1.5 fusion.86
  504.7 1.5 fusion.86
  506.1 2.3 multiply_reduce_fusion.1
  509.9 3.3 fusion.14
  514.4 3.4 convolution_bitcast_fusion.2
  517.8 3.8 fusion.9
  521.6 1.6 copy.70
  523.2 1.6 multiply_multiply_fusion
  527.4 110.9 %all-gather.17.cloned.1.call-done = f32[256,128,128]{2,1,0:T(8,128)} async-done(((f32[16,128,128]{2,1,0:T(8,128)}), f32[256,128,128]{2,1,0:T(8,128)}) %all-gather.17.cloned.1.call-update) | async-done | bytes 16777232 | tf_op jit(solution)/shard_map/all_gather | solution.py:13
  638.4 11.6 %rev.7 = f32[16,16,128,128]{3,2,1,0:T(8,128)} reverse(f32[16,16,128,128]{3,2,1,0:T(8,128)} %bitcast.143), dimensions={0} | reverse | bytes 33554432 | tf_op jit(solution)/shard_map/rev | solution.py:15
  650.0 22.6 %while.29 = (s32[]{:T(128)}, f32[16,128,128]{2,1,0:T(8,128)S(1)}, s32[]{:T(128)}, f32[16,16]{1,0:T(8,128)S(1)}, f32[16,16,128,128]{3,2,1,0:T(8,128)}, /*index=5*/s32[]{:T(128)}, s32[]{:T(128)}) while((s32[]{:T(128)}, f32[16,128,128]{2,1,0:T(8,128)S(1)}, s32[]{:T(128)}, f32[16,16]{1,0:T(8,128)S(1)}, f32[16,16,128,128]{3,2,1,0:T(8,128)}, ...), condition=%wide.region_6.7_spmd.clone, body=%wide.region_5.6_spmd.clone.sunk | while | flops 1048580 | bytes 3146025 | solution.py:25
  650.0 1.6 fusion.87
  651.6 1.5 fusion.87
  654.6 1.5 fusion.87
  656.1 1.5 fusion.87
  659.1 1.5 fusion.87
  660.6 1.5 fusion.87
  663.6 1.5 fusion.87
  673.6 1.6 fusion.7
  679.6 2.1 pad_maximum_fusion
  682.5 16.2 %all-reduce.4.cloned.1.call-done = f32[128,128]{0,1:T(8,128)} async-done(((f32[128,128]{0,1:T(8,128)}), f32[128,128]{0,1:T(8,128)}) %all-reduce.4.cloned.1.call-update) | async-done | bytes 65552 | tf_op jit(solution)/shard_map/psum | solution.py:157
  698.7 2.3 fusion.55
  701.0 95.1 %all-reduce.6.cloned.1.call-done = f32[2,64,2048]{2,1,0:T(8,128)} async-done(((f32[2,64,2048]{2,1,0:T(8,128)}), f32[2,64,2048]{2,1,0:T(8,128)}) %all-reduce.6.cloned.1.call-update) | async-done | bytes 1048592 | tf_op jit(solution)/shard_map/psum | solution.py:138
  796.2 60.4 %reduce-scatter.2.cloned.1.call-done = f32[112,128]{1,0:T(8,128)} async-done(((f32[1792,128]{1,0:T(8,128)}), f32[112,128]{1,0:T(8,128)}) %reduce-scatter.2.cloned.1.call-update) | async-done | bytes 57360 | tf_op jit(solution)/shard_map/reduce_scatter | solution.py:163
  856.6 2.3 copy.115
  (118 shorter events, 38.9 us)
Async XLA Ops:
  7.2 4.5 copy-start
  7.2 234.1 %copy-start.2 = (bf16[128,3584]{1,0:T(8,128)(2,1)S(1)}, bf16[128,3584]{1,0:T(8,128)(2,1)}, u32[]{:S(2)}) copy-start(bf16[128,3584]{1,0:T(8,128)(2,1)} %param.12) | copy-start | bytes 2752516
  7.2 127.3 %copy-start.8 = (bf16[2,64,2048]{2,1,0:T(8,128)(2,1)S(1)}, bf16[2,64,2048]{2,1,0:T(8,128)(2,1)}, u32[]{:S(2)}) copy-start(bf16[2,64,2048]{2,1,0:T(8,128)(2,1)} %param.17) | copy-start | bytes 1572868
  7.2 119.7 %all-gather.13.cloned.1.call-start = ((), (), s32[]{:S(2)}) async-start(), calls=%async_computation.3 | async-start | bytes 15597568 | tf_op jit(solution)/shard_map/all_gather | solution.py:69
  7.9 233.3 %all-gather.11.cloned.1.call-start = ((), (), s32[]{:S(2)}) async-start(), calls=%async_computation.2 | async-start | bytes 15597568 | tf_op jit(solution)/shard_map/all_gather | solution.py:68
  8.7 347.3 %all-gather.9.cloned.1.call-start = ((), (), s32[]{:S(2)}) async-start(), calls=%async_computation.1 | async-start | bytes 15597568 | tf_op jit(solution)/shard_map/all_gather | solution.py:67
  9.4 474.2 %all-gather.15.cloned.1.call-start = ((), (), s32[]{:S(2)}) async-start(), calls=%async_computation.7 | async-start | bytes 17825792 | tf_op jit(solution)/shard_map/all_gather | solution.py:13
  10.4 0.6 copy-start.12
  13.3 235.3 %copy-start.10 = (bf16[128,128]{0,1:T(8,128)(2,1)}, bf16[128,128]{0,1:T(8,128)(2,1)S(1)}, u32[]{:S(2)}) copy-start(bf16[128,128]{0,1:T(8,128)(2,1)S(1)} %convolution_convert_fusion) | copy-start | bytes 98308
  134.8 152.1 %copy-start.6 = (bf16[128,2048]{1,0:T(8,128)(2,1)}, bf16[128,2048]{1,0:T(8,128)(2,1)S(1)}, u32[]{:S(2)}) copy-start(bf16[128,2048]{1,0:T(8,128)(2,1)S(1)} %fusion.4) | copy-start | bytes 1572868
  134.8 116.2 %copy-start.15 = (u32[32]{0:T(128)S(1)}, u32[32]{0:T(128)}, u32[]{:S(2)}) copy-start(u32[32]{0:T(128)} %constant.84) | copy-start | bytes 388
  248.6 114.6 %copy-start.11 = (bf16[128,128]{0,1:T(8,128)(2,1)S(1)}, bf16[128,128]{0,1:T(8,128)(2,1)}, u32[]{:S(2)}) copy-start(bf16[128,128]{0,1:T(8,128)(2,1)} %copy-done.10) | copy-start | bytes 98308
  250.9 387.4 %all-gather.17.cloned.1.call-start = ((), (), s32[]{:S(2)}) async-start(), calls=%async_computation.8 | async-start | bytes 17825792 | tf_op jit(solution)/shard_map/all_gather | solution.py:13
  286.9 81.5 %copy-start.13 = (f32[16,128]{1,0:T(8,128)S(1)}, f32[16,128]{1,0:T(8,128)}, u32[]{:S(2)}) copy-start(f32[16,128]{1,0:T(8,128)} %copy-done.12) | copy-start | bytes 24580
  363.2 145.2 %copy-start.5 = (f32[128,2048]{0,1:T(8,128)S(1)}, f32[128,2048]{0,1:T(8,128)}, u32[]{:S(2)}) copy-start(f32[128,2048]{0,1:T(8,128)} %copy.40) | copy-start | bytes 3145732
  369.1 0.8 copy-start.7
  483.7 34.1 %copy-start.14 = (f32[128,16]{0,1:T(8,128)S(1)}, f32[128,16]{0,1:T(8,128)}, u32[]{:S(2)}) copy-start(f32[128,16]{0,1:T(8,128)} %get-tuple-element.250) | copy-start | bytes 24580
  508.9 1.0 copy-start.4
  513.1 13.0 %copy-start.9 = (bf16[2,64,2048]{2,1,0:T(8,128)(2,1)S(1)}, bf16[2,64,2048]{2,1,0:T(8,128)(2,1)}, u32[]{:S(2)}) copy-start(bf16[2,64,2048]{2,1,0:T(8,128)(2,1)} %param.17) | copy-start | bytes 1572868
  513.1 185.5 %all-reduce.4.cloned.1.call-start = ((), (), s32[]{:S(2)}) async-start(), calls=%async_computation.4 | async-start | bytes 131072 | tf_op jit(solution)/shard_map/psum | solution.py:157
  650.0 31.8 %copy-start.3 = (bf16[128,3584]{1,0:T(8,128)(2,1)S(1)}, bf16[128,3584]{1,0:T(8,128)(2,1)}, u32[]{:S(2)}) copy-start(bf16[128,3584]{1,0:T(8,128)(2,1)} %param.12) | copy-start | bytes 2752516
  650.0 208.9 %copy-start.1 = (bf16[3584,128]{1,0:T(8,128)(2,1)S(1)}, bf16[3584,128]{1,0:T(8,128)(2,1)}, u32[]{:S(2)}) copy-start(bf16[3584,128]{1,0:T(8,128)(2,1)} %param.16) | copy-start | bytes 2752516
  679.6 116.6 %all-reduce.6.cloned.1.call-start = ((), (), s32[]{:S(2)}) async-start(), calls=%async_computation.6 | async-start | bytes 2097152 | tf_op jit(solution)/shard_map/psum | solution.py:138
  681.8 174.8 %reduce-scatter.2.cloned.1.call-start = ((), (), s32[]{:S(2)}) async-start(), calls=%async_computation.5 | async-start | bytes 974848 | tf_op jit(solution)/shard_map/reduce_scatter | solution.py:163
Sparse Core Ops, SparseCore 0:
  10.3 116.5 all-gather.12
  129.2 112.0 all-gather.10
  243.6 112.3 all-gather.8
  358.6 125.0 all-gather.14
  513.3 125.0 all-gather.16
  679.7 18.9 all-reduce.3
  702.7 93.3 all-reduce.5
  800.3 56.2 reduce-scatter.1
where the time goes:
time: 868 us; the launch traced here: 866 us
  waiting for transfers between devices  686 us (79%)
  matrix products  54.4 us (6%)
  other arithmetic  51 us (6%)
  blocking collectives  32 us (4%)
  local copies, waits for them, and re-layouts  25.6 us (3%)
  between operations  15.2 us (2%)
    all_gather x2, waiting for transfers between devices, carried_in(): pieces = jax.tree.map(lambda part: lax.all_gather(part, axis), value)  223 us
    all_gather x1, waiting for transfers between devices, on_device(): lax.all_gather(value_weight, 'seq', axis=0, tiled=True)  114 us
    all_gather x1, waiting for transfers between devices, on_device(): lax.all_gather(key_weight, 'seq', axis=0, tiled=True)  106 us
    psum x1, waiting for transfers between devices, on_device(): grad_up = lax.psum(up_products, 'seq')  95.1 us
    all_gather x1, waiting for transfers between devices, on_device(): lax.all_gather(query_weight, 'seq', axis=0, tiled=True)  69 us
    reduce_scatter x1, waiting for transfers between devices, on_device(): lax.psum_scatter(jnp.dot(columns.T, whole_low, precision=exact_arithmetic...  60.4 us
    select_n x30, other arithmetic, hop(): jnp.where(position < mine, new, old)  43.9 us
    unnamed x1, blocking collectives  32 us
  transfers between devices with their start and end apart: 8, of which 8 were waited for; matrix products, arithmetic and copies ran while one was open for 7% of the time, Pallas kernels for 0%

commit v1 on v0

--- a/solution.py
+++ b/solution.py
@@ -1,6 +1,10 @@
+import functools
+
 import jax
 import jax.numpy as jnp
 from jax import lax
+from jax.experimental import pallas as pl
+from jax.experimental.pallas import tpu as pltpu
 from jax.sharding import PartitionSpec as P
 
 adapter_scale = 2.0
@@ -169,9 +173,178 @@
     return (grad_down, grad_up)
 
 
+def dot_f32(a, b, contract):
+    return lax.dot_general(a, b, ((contract[:1], contract[1:]), ((), ())), preferred_element_type=jnp.float32)
+
+
+def layer_kernel(
+    rank,
+    tokens_ref,
+    weight_ref,
+    lift_ref,
+    cumulative_ref,
+    upstream_ref,
+    low_grad_ref,
+    up_ref,
+    state,
+    low_all,
+    key_all,
+    carried_all,
+    grads,
+):
+    step = pl.program_id(0)
+    steps = pl.num_programs(0)
+    length = tokens_ref.shape[0]
+    size = state.shape[0]
+    half = jnp.bfloat16
+
+    def decays(block):
+        row = jnp.broadcast_to(cumulative_ref[pl.ds(block, 1), :], (length, length))
+        column = row.T
+        last = row[:, length - 1 :]
+        return row, column, jnp.broadcast_to(last, (length, length))
+
+    @pl.when(step == 0)
+    def _():
+        state[...] = jnp.zeros_like(state)
+
+    product = jnp.dot(tokens_ref[...], weight_ref[...], preferred_element_type=jnp.float32)
+    low = product[:, 3 * size :].astype(half)
+    lifted = jnp.dot(low, lift_ref[...], preferred_element_type=jnp.float32)
+    query_pre = product[:, :size] + lifted[:, :size]
+    key_pre = product[:, size : 2 * size]
+    value = (product[:, 2 * size : 3 * size] + lifted[:, size:]).astype(half)
+    sig = jax.nn.sigmoid(query_pre)
+    query = (query_pre * sig).astype(half)
+    key = (key_pre * jax.nn.sigmoid(key_pre)).astype(half)
+    row, column, total = decays(step)
+    causal = lax.broadcasted_iota(jnp.int32, (length, length), 0) >= lax.broadcasted_iota(
+        jnp.int32, (length, length), 1
+    )
+    decay_mat = jnp.where(causal, jnp.exp(jnp.where(causal, column - row, 0.0)), 0.0)
+    lead = jnp.exp(column)
+    tail = jnp.exp(total - column)
+    held = state[...]
+    held_half = held.astype(half)
+    mixed = (dot_f32(query, key, (1, 1)) * decay_mat).astype(half)
+    attn = dot_f32(mixed, value, (1, 0)) + lead * dot_f32(query, held_half, (1, 0))
+    rms = jnp.sqrt(jnp.mean(attn * attn, axis=-1, keepdims=True) + eps_norm)
+    normed = attn / rms
+    upstream = upstream_ref[...].astype(jnp.float32)
+    d_attn = (upstream - normed * jnp.mean(upstream * normed, axis=-1, keepdims=True)) / rms
+    d_attn_b = d_attn.astype(half)
+    carried_all[step] = dot_f32((query.astype(jnp.float32) * lead).astype(half), d_attn_b, (0, 0))
+    d_mixed = (dot_f32(d_attn_b, value, (1, 1)) * decay_mat).astype(half)
+    d_query = dot_f32(d_mixed, key, (1, 0)) + lead * dot_f32(d_attn_b, held_half, (1, 1))
+    d_query_pre = d_query * (sig * (1.0 + query_pre * (1.0 - sig)))
+    d_value = dot_f32(mixed, d_attn_b, (0, 0))
+    gain = jnp.exp(total)
+    state[...] = gain[:1, :] * held + dot_f32((key.astype(jnp.float32) * tail).astype(half), value, (0, 0))
+    rows = pl.ds(pl.multiple_of(step * length, length), length)
+    low_all[rows, :] = low
+    key_all[rows, :] = key
+    grads[rows, :size] = d_query_pre
+    grads[rows, size:] = d_value
+
+    @pl.when(step == steps - 1)
+    def _():
+        def back(i, later):
+            block = steps - 1 - i
+            at = pl.ds(pl.multiple_of(block * length, length), length)
+            _, column, total = decays(block)
+            tail = jnp.exp(total - column)
+            grads[at, size:] += tail * dot_f32(key_all[at, :], later.astype(half), (1, 0))
+            return carried_all[block] + jnp.exp(total)[:1, :] * later
+
+        lax.fori_loop(0, steps, back, jnp.zeros(state.shape, jnp.float32))
+        both = grads[...].astype(half)
+        low_grad_ref[...] = dot_f32(both, lift_ref[...], (1, 1))
+        ups = dot_f32(low_all[...], both, (0, 0))
+        up_ref[0] = adapter_scale * ups[:rank, :size]
+        up_ref[1] = adapter_scale * ups[rank:, size:]
+
+
+def head_on_device(
+    tokens,
+    query_weight,
+    key_weight,
+    value_weight,
+    adapter_down_maps,
+    lifting_matrices,
+    decay_logarithms,
+    output_gradient,
+):
+    seq_count = lax.axis_size("seq")
+    model_count = lax.axis_size("mp")
+    length, width = tokens.shape
+    heads = decay_logarithms.shape[0]
+    size = query_weight.shape[1] // heads
+    rank = lifting_matrices.shape[1]
+    tokens_all = lax.all_gather(tokens, "seq", axis=0, tiled=True)
+    weights = jnp.stack([query_weight, key_weight, value_weight])
+    weights = lax.all_to_all(weights, "seq", split_axis=2, concat_axis=1, tiled=True)
+    upstream = lax.all_to_all(output_gradient, "seq", split_axis=1, concat_axis=0, tiled=True)
+    cumulative = jnp.cumsum(decay_logarithms, axis=1)
+    cumulative = lax.all_to_all(cumulative, "seq", split_axis=0, concat_axis=1, tiled=True)
+    cumulative = cumulative.reshape(seq_count, length)
+    weight = jnp.concatenate([weights[0], weights[1], weights[2], adapter_down_maps], axis=1)
+    lift = lax.dynamic_slice_in_dim(lifting_matrices, lax.axis_index("seq") * size, size, 2)
+    lift = (adapter_scale * lift).astype(jnp.bfloat16)
+    empty = jnp.zeros_like(lift[0])
+    lift = jnp.concatenate(
+        [jnp.concatenate([lift[0], empty], axis=1), jnp.concatenate([empty, lift[1]], axis=1)], axis=0
+    )
+    total_tokens = length * seq_count
+    low_gradient, up_products = pl.pallas_call(
+        functools.partial(layer_kernel, rank),
+        grid=(seq_count,),
+        out_shape=(
+            jax.ShapeDtypeStruct((total_tokens, 2 * rank), jnp.float32),
+            jax.ShapeDtypeStruct((2, rank, size), jnp.float32),
+        ),
+        in_specs=[
+            pl.BlockSpec((length, width), lambda i: (i, 0)),
+            pl.BlockSpec(weight.shape, lambda i: (0, 0)),
+            pl.BlockSpec(lift.shape, lambda i: (0, 0)),
+            pl.BlockSpec(cumulative.shape, lambda i: (0, 0)),
+            pl.BlockSpec((length, size), lambda i: (i, 0)),
+        ],
+        out_specs=(
+            pl.BlockSpec((total_tokens, 2 * rank), lambda i: (0, 0)),
+            pl.BlockSpec((2, rank, size), lambda i: (0, 0, 0)),
+        ),
+        scratch_shapes=[
+            pltpu.VMEM((size, size), jnp.float32),
+            pltpu.VMEM((total_tokens, 2 * rank), jnp.bfloat16),
+            pltpu.VMEM((total_tokens, size), jnp.bfloat16),
+            pltpu.VMEM((seq_count, size, size), jnp.float32),
+            pltpu.VMEM((total_tokens, 2 * size), jnp.float32),
+        ],
+        compiler_params=pltpu.CompilerParams(
+            dimension_semantics=("arbitrary",), vmem_limit_bytes=48 * 1024 * 1024
+        ),
+    )(tokens_all, weight, lift, cumulative, upstream)
+    grad_up = lax.all_gather(up_products, "seq", axis=2, tiled=True)
+    whole_low = lax.psum(low_gradient, ("seq", "mp"))
+    own_rows = width // (seq_count * model_count)
+    place = lax.axis_index("seq") * model_count + lax.axis_index("mp")
+    mine = lax.dynamic_slice_in_dim(tokens_all, place * own_rows, own_rows, 1)
+    grad_down = lax.dot_general(
+        mine, whole_low.astype(jnp.bfloat16), (((0,), (0,)), ((), ())), preferred_element_type=jnp.float32
+    )
+    return (grad_down, grad_up)
+
+
+def per_device(*arrays):
+    decay = arrays[6]
+    one_head = decay.shape[0] == lax.axis_size("seq")
+    square = decay.shape[1] == arrays[1].shape[1] // decay.shape[0]
+    return (head_on_device if one_head and square else on_device)(*arrays)
+
+
 def solution(mesh):
     return jax.shard_map(
-        on_device,
+        per_device,
         mesh=mesh,
         in_specs=(
             P("seq", None),

time: 868 us -> 317 us (0.37)
  waiting for transfers between devices: 686 us -> 140 us
  starting transfers between devices: 0.54 us -> 53.3 us
  matrix products: 54.4 us -> 2.36 us
  other arithmetic: 51 us -> 6.43 us
  Pallas kernels: 0 us -> 27.9 us
  blocking collectives: 32 us -> 52.7 us
    all_gather x5 -> x2, waiting for transfers between devices: 512 us -> 0.01 us  [the longest x1 0.01 us: head_on_device(): tokens_all = lax.all_gather(tokens, 'seq', axis=0, tiled=True)]
    all_to_all x0 -> x3, waiting for transfers between devices: none -> 139 us  [the longest x1 136 us: head_on_device(): lax.all_to_all(weights, 'seq', split_axis=2, concat_axis=1, tiled=True)]
    psum x2 -> x0, waiting for transfers between devices: 111 us -> none  [the longest x1 95.1 us: on_device(): grad_up = lax.psum(up_products, 'seq')]
    reduce_scatter x1 -> x0, waiting for transfers between devices: 60.4 us -> none  [on_device(): lax.psum_scatter(jnp.dot(columns.T, whole_low, precision=exact_arithmetic...]
    all_to_all x0 -> x3, starting transfers between devices: none -> 53.2 us  [the longest x1 39.8 us: head_on_device(): lax.all_to_all(output_gradient, 'seq', split_axis=1, concat_axis=0, tiled...]
    psum x0 -> x1, blocking collectives: none -> 52.7 us  [head_on_device(): whole_low = lax.psum(low_gradient, ('seq', 'mp'))]
    dot_general x20 -> x1, matrix products: 54.4 us -> 2.36 us  [head_on_device(): lax.dot_general(mine, whole_low.astype(jnp.bfloat16), (((0,), (0,)), ((),...]
    select_n x30 -> x0, other arithmetic: 43.9 us -> none  [hop(): jnp.where(position < mine, new, old)]
  transfers between devices with their start and end apart: 8 -> 5, of which waited for: 8 -> 2; matrix products, arithmetic and copies ran while one was open for 7% -> 7% of each run, Pallas kernels for 0% -> 0%
where the time goes in v1:
time: 317 us; the launch traced here: 316 us
  waiting for transfers between devices  140 us (44%)
  starting transfers between devices  53.3 us (17%)
  blocking collectives  52.7 us (17%)
  Pallas kernels  27.9 us (9%)
  local copies, waits for them, and re-layouts  19.1 us (6%)
  between operations  14.1 us (4%)
  other arithmetic  6.43 us (2%)
    all_to_all x1, waiting for transfers between devices, head_on_device(): lax.all_to_all(weights, 'seq', split_axis=2, concat_axis=1, tiled=True)  136 us
    psum x1, blocking collectives, head_on_device(): whole_low = lax.psum(low_gradient, ('seq', 'mp'))  52.7 us
    all_to_all x1, starting transfers between devices, head_on_device(): lax.all_to_all(output_gradient, 'seq', split_axis=1, concat_axis=0, tiled...  39.8 us
    pallas_call x1, Pallas kernels, head_on_device(): pl.pallas_call(functools.partial(layer_kernel, rank), grid=(seq_count,),...  27.9 us
    all_to_all x1, starting transfers between devices, head_on_device(): lax.all_to_all(cumulative, 'seq', split_axis=0, concat_axis=1, tiled=True)  7.39 us
    all_to_all x1, local copies, waits for them, and re-layouts, head_on_device(): lax.all_to_all(weights, 'seq', split_axis=2, concat_axis=1, tiled=True)  7.02 us
  transfers between devices with their start and end apart: 5, of which 2 were waited for; matrix products, arithmetic and copies ran while one was open for 7% of the time, Pallas kernels for 0%

profile of v1, /device:TPU:0, one launch (start us, length us, event | category | flops | bytes accessed | tf_op | source)
XLA Modules:
  0.0 315.8 jit_solution(13750710943000626022)
XLA Ops:
  7.2 0.0 copy-start
  7.2 0.0 all-gather.3.cloned.1.call-start
  7.2 0.7 all-gather.3.cloned.1.call-update
  7.9 1.6 reduce_window_sum.14
  9.5 7.4 %all-to-all-start.1 = ((f32[16,1,128]{2,1,0:T(1,128)}), f32[16,1,128]{2,1,0:T(1,128)S(1)}, u32[]{:S(2)}, u32[]{:S(2)}) async-start(f32[16,1,128]{2,1,0:T(1,128)} %bitcast.11), calls=%async_computation.1 | async-start | bytes 16384 | tf_op jit(solution)/shard_map/all_to_all | solution.py:288
  16.9 2.0 pad_maximum_fusion.1
  18.9 4.8 %copy.18 = bf16[3,224,2048]{1,0,2:T(4,128)(2,1)} copy(bf16[3,224,2048]{2,1,0:T(8,128)(2,1)S(1)} %pad_maximum_fusion.1) | data formatting | bytes 5505024 | tf_op jit(solution)/shard_map/stack | solution.py:284
  23.7 0.0 all-to-all-done.1
  23.7 6.1 %all-to-all-start = ((bf16[3,224,2048]{1,0,2:T(4,128)(2,1)}), bf16[3,224,2048]{1,0,2:T(4,128)(2,1)}, u32[]{:S(2)}, u32[]{:S(2)}) async-start(bf16[3,224,2048]{1,0,2:T(4,128)(2,1)} %copy.18), calls=%async_computation | async-start | bytes 8388608 | tf_op jit(solution)/shard_map/all_to_all | solution.py:285
  29.8 0.8 dynamic-slice_multiply_fusion
  30.5 0.0 copy-done
  30.6 0.9 copy_bitcast_fusion
  31.5 135.9 %all-to-all-done = bf16[3,224,2048]{1,0,2:T(4,128)(2,1)} async-done(((bf16[3,224,2048]{1,0,2:T(4,128)(2,1)}), bf16[3,224,2048]{1,0,2:T(4,128)(2,1)}, u32[]{:S(2)}, u32[]{:S(2)}) %all-to-all-start) | async-done | bytes 2752544 | tf_op jit(solution)/shard_map/all_to_all | solution.py:285
  167.4 39.8 %all-to-all-start.2 = ((bf16[128,16,128]{2,0,1:T(8,128)(2,1)}), bf16[128,16,128]{2,0,1:T(8,128)(2,1)S(1)}, u32[]{:S(2)}, u32[]{:S(2)}) async-start(bf16[128,16,128]{2,0,1:T(8,128)(2,1)} %copy_bitcast_fusion), calls=%async_computation.2 | async-start | bytes 1048576 | tf_op jit(solution)/shard_map/all_to_all | solution.py:286
  207.1 0.0 all-gather.5.cloned.1.call-start
  207.2 7.0 %copy.19 = bf16[3,224,16,128]{3,1,2,0:T(8,128)(2,1)} copy(bf16[3,224,16,128]{1,0,3,2:T(4,128)(2,1)} %bitcast.3) | data formatting | bytes 5505024 | tf_op jit(solution)/shard_map/all_to_all | solution.py:285
  214.2 0.0 copy-start.2
  214.2 2.0 fusion.7
  216.2 0.0 copy-done.2
  216.2 2.0 pad_maximum_fusion.weight_ref
  218.3 3.3 %all-to-all-done.2 = bf16[128,16,128]{2,0,1:T(8,128)(2,1)S(1)} async-done(((bf16[128,16,128]{2,0,1:T(8,128)(2,1)}), bf16[128,16,128]{2,0,1:T(8,128)(2,1)S(1)}, u32[]{:S(2)}, u32[]{:S(2)}) %all-to-all-start.2) | async-done | bytes 524320 | tf_op jit(solution)/shard_map/all_to_all | solution.py:286
  221.6 0.0 all-gather.3.cloned.1.call-done.tokens_ref
  221.6 0.0 copy-start.1
  221.6 2.0 copy-done.1
  223.6 27.9 %shard_map.95 = (f32[2048,128]{1,0:T(8,128)S(1)}, f32[2,64,128]{2,1,0:T(8,128)}) custom-call(bf16[2048,3584]{1,0:T(8,128)(2,1)} %all-gather.3.cloned.1.call-done.tokens_ref, bf16[3584,512]{1,0:T(8,128)(2,1)S(1)} %copy-done.1, bf16[128,256]{1,0:T(8,128)(2,1)S(1)} %fusion.5.lift_ref, f32[16,128]{1,0:T(8,128)S(1)} %bitcast.25, bf16[2048,128]{1,0:T(8,128)(2,1)S(1)} %bitcast.24), custom_call_target="tpu_custom_call" | custom-call | tf_op jit(solution)/shard_map/pallas_call | solution.py:298
  251.6 0.0 all-gather.5.cloned.1.call-update
  251.6 52.7 %all-reduce.3 = bf16[2048,128]{1,0:T(8,128)(2,1)S(1)} all-reduce(f32[2048,128]{1,0:T(8,128)S(1)} %get-tuple-element.4), channel_id=1, replica_groups=mesh['seq'=16,'mp'=2] {'seq','mp'}, use_global_device_ids=true, to_apply=%region_1.2 | all-reduce | flops 262144 | bytes 1572864 | tf_op jit(solution)/shard_map/psum | solution.py:328
  304.3 2.4 fusion
  306.7 0.0 all-gather.5.cloned.1.call-done
  306.7 2.3 copy.27
  (2 shorter events, 0.0 us)
Async XLA Ops:
  7.2 23.4 %copy-start = (bf16[128,2048]{1,0:T(8,128)(2,1)S(1)}, bf16[128,2048]{1,0:T(8,128)(2,1)}, u32[]{:S(2)}) copy-start(bf16[128,2048]{1,0:T(8,128)(2,1)} %param.15) | copy-start | bytes 1572868
  7.2 214.4 %all-gather.3.cloned.1.call-start = ((), (), s32[]{:S(2)}) async-start(), calls=%async_computation.3 | async-start | bytes 15597568 | tf_op jit(solution)/shard_map/all_gather | solution.py:283
  9.5 14.2 %all-to-all-start.1 = ((f32[16,1,128]{2,1,0:T(1,128)}), f32[16,1,128]{2,1,0:T(1,128)S(1)}, u32[]{:S(2)}, u32[]{:S(2)}) async-start(f32[16,1,128]{2,1,0:T(1,128)} %bitcast.11), calls=%async_computation.1 | async-start | bytes 16384 | tf_op jit(solution)/shard_map/all_to_all | solution.py:288
  23.7 143.7 %all-to-all-start = ((bf16[3,224,2048]{1,0,2:T(4,128)(2,1)}), bf16[3,224,2048]{1,0,2:T(4,128)(2,1)}, u32[]{:S(2)}, u32[]{:S(2)}) async-start(bf16[3,224,2048]{1,0,2:T(4,128)(2,1)} %copy.18), calls=%async_computation | async-start | bytes 8388608 | tf_op jit(solution)/shard_map/all_to_all | solution.py:285
  167.4 54.2 %all-to-all-start.2 = ((bf16[128,16,128]{2,0,1:T(8,128)(2,1)}), bf16[128,16,128]{2,0,1:T(8,128)(2,1)S(1)}, u32[]{:S(2)}, u32[]{:S(2)}) async-start(bf16[128,16,128]{2,0,1:T(8,128)(2,1)} %copy_bitcast_fusion), calls=%async_computation.2 | async-start | bytes 1048576 | tf_op jit(solution)/shard_map/all_to_all | solution.py:286
  207.1 99.5 %all-gather.5.cloned.1.call-start = ((), (), s32[]{:S(2)}) async-start(), calls=%async_computation.4 | async-start | bytes 1114112 | tf_op jit(solution)/shard_map/all_gather | solution.py:327
  214.2 2.0 copy-start.2
  221.6 2.0 copy-start.1
Sparse Core Ops, SparseCore 0:
  10.3 193.0 all-gather.2
  251.7 37.3 all-gather.4

commit v2 on v1

--- a/solution.py
+++ b/solution.py
@@ -199,7 +199,8 @@
     half = jnp.bfloat16
 
     def decays(block):
-        row = jnp.broadcast_to(cumulative_ref[pl.ds(block, 1), :], (length, length))
+        at = block * steps + lax.axis_index("seq")
+        row = jnp.broadcast_to(cumulative_ref[pl.ds(at, 1), :], (length, length))
         column = row.T
         last = row[:, length - 1 :]
         return row, column, jnp.broadcast_to(last, (length, length))
@@ -258,10 +259,296 @@
 
         lax.fori_loop(0, steps, back, jnp.zeros(state.shape, jnp.float32))
         both = grads[...].astype(half)
-        low_grad_ref[...] = dot_f32(both, lift_ref[...], (1, 1))
+        low_grad_ref[...] = dot_f32(both, lift_ref[...], (1, 1)).astype(half)
         ups = dot_f32(low_all[...], both, (0, 0))
         up_ref[0] = adapter_scale * ups[:rank, :size]
         up_ref[1] = adapter_scale * ups[rank:, size:]
+
+
+MESH = pl.DeviceIdType.MESH
+
+
+def exchange_kernel(
+    tokens_ref,
+    query_ref,
+    key_ref,
+    value_ref,
+    down_ref,
+    upstream_ref,
+    cumulative_ref,
+    tokens_all,
+    weight_all,
+    upstream_all,
+    cumulative_all,
+    local_sem,
+    token_send,
+    token_recv,
+    block_send,
+    block_recv,
+):
+    count = lax.axis_size("seq")
+    me, x = lax.axis_index("seq"), lax.axis_index("mp")
+    core, y, z = lax.rem(me, 2), lax.rem(me // 2, 2), me // 4
+    layers = count // 4
+    length = tokens_ref.shape[0]
+    half = length // 2
+    depth = query_ref.shape[0]
+    size = upstream_all.shape[1]
+    heads = cumulative_ref.shape[0]
+    barrier = pltpu.get_barrier_semaphore()
+
+    def greet(j, carry):
+        pl.semaphore_signal(
+            barrier, inc=1, device_id=(lax.rem(me + j, count), x), device_id_type=MESH
+        )
+        return carry
+
+    lax.fori_loop(1, count, greet, 0)
+    pl.semaphore_signal(barrier, inc=1, device_id=(me, 1 - x), device_id_type=MESH)
+    pl.semaphore_wait(barrier, count)
+
+    def seq_of(zz, yy, cc):
+        return (zz * 2 + yy) * 2 + cc
+
+    def rows_of(block, part):
+        return pl.ds(pl.multiple_of(block * length + part * half, half), half)
+
+    sent = []
+
+    def send(block, part, device, own=False):
+        source = (
+            tokens_ref.at[pl.ds(pl.multiple_of(part * half, half), half), :]
+            if own
+            else tokens_all.at[rows_of(block, part), :]
+        )
+        copy = pltpu.make_async_remote_copy(
+            src_ref=source,
+            dst_ref=tokens_all.at[rows_of(block, part), :],
+            send_sem=token_send.at[len(sent)],
+            recv_sem=token_recv.at[block * 2 + part],
+            device_id=device,
+            device_id_type=MESH,
+        )
+        copy.start()
+        sent.append(copy)
+
+    def arrived(block, part):
+        at = tokens_all.at[rows_of(block, part), :]
+        pltpu.make_async_copy(at, at, token_recv.at[block * 2 + part]).wait()
+
+    over_y = (seq_of(z, 1 - y, core), x)
+    over_x = (me, 1 - x)
+    sibling = (seq_of(z, y, 1 - core), x)
+    weights = (query_ref, key_ref, value_ref)
+
+    def block_copies(j, source, target):
+        to = (target, x)
+        pairs = [
+            (
+                weight.at[:, pl.ds(pl.multiple_of(target * size, size), size)],
+                weight_all.at[
+                    pl.ds(pl.multiple_of(source * depth, depth), depth), k * size : (k + 1) * size
+                ],
+            )
+            for k, weight in enumerate(weights)
+        ]
+        pairs.append(
+            (
+                upstream_ref.at[:, pl.ds(pl.multiple_of(target * size, size), size)],
+                upstream_all.at[pl.ds(pl.multiple_of(source * length, length), length), :],
+            )
+        )
+        pairs.append(
+            (
+                cumulative_ref,
+                cumulative_all.at[pl.ds(pl.multiple_of(source * heads, heads), heads), :],
+            )
+        )
+        return [
+            pltpu.make_async_remote_copy(
+                src_ref=source_ref,
+                dst_ref=dst_ref,
+                send_sem=block_send.at[k, j],
+                recv_sem=block_recv.at[k, j],
+                device_id=to,
+                device_id_type=MESH,
+            )
+            for k, (source_ref, dst_ref) in enumerate(pairs)
+        ], pairs
+
+    for j in range(1, layers):
+        send(me, x, (seq_of(lax.rem(z + j, layers), y, core), x), own=True)
+    send(me, x, over_y, own=True)
+    send(me, 0, sibling, own=True)
+    send(me, 1, sibling, own=True)
+
+    def start_blocks(j, carry):
+        for copy in block_copies(j, me, lax.rem(me + j, count))[0]:
+            copy.start()
+        return carry
+
+    lax.fori_loop(1, count, start_blocks, 0)
+    mine = [(tokens_ref, tokens_all.at[pl.ds(pl.multiple_of(me * length, length), length), :])]
+    mine += block_copies(0, me, me)[1]
+    mine.append((down_ref, weight_all.at[:, 3 * size :]))
+    local = [
+        pltpu.make_async_copy(a, b, local_sem.at[k]) for k, (a, b) in enumerate(mine)
+    ]
+    for copy in local:
+        copy.start()
+
+    def along_z(j):
+        block = seq_of(lax.rem(z - j + layers, layers), y, core)
+        arrived(block, x)
+        send(block, x, over_y)
+        send(block, x, over_x)
+        send(block, x, sibling)
+
+    def along_y(j):
+        block = seq_of(lax.rem(z - j + layers, layers), 1 - y, core)
+        arrived(block, x)
+        send(block, x, over_x)
+        send(block, x, sibling)
+
+    def along_x(j):
+        for other in range(2) if j else (1,):
+            yy = 1 - y if other else y
+            block = seq_of(lax.rem(z - j + layers, layers), yy, core)
+            arrived(block, 1 - x)
+            send(block, 1 - x, sibling)
+
+    for step in range(layers + 2):
+        if 1 <= step + 1 < layers:
+            along_z(step + 1)
+        if step < layers:
+            along_y(step)
+        if 0 <= step - 1 < layers:
+            along_x(step - 1)
+    for zz in range(layers):
+        for yy in range(2):
+            for part in range(2):
+                arrived(seq_of(zz, yy, 1 - core), part)
+
+    def end_blocks(j, carry):
+        source = lax.rem(me - j + count, count)
+        for copy in block_copies(j, source, me)[0]:
+            copy.wait_recv()
+        for copy in block_copies(j, me, lax.rem(me + j, count))[0]:
+            copy.wait_send()
+        return carry
+
+    lax.fori_loop(1, count, end_blocks, 0)
+    for copy in local:
+        copy.wait()
+    for copy in sent:
+        copy.wait_send()
+
+
+def reduce_kernel(
+    low_ref,
+    up_ref,
+    tokens_all,
+    down_out,
+    up_out,
+    pieces,
+    whole,
+    window,
+    product,
+    window_sem,
+    piece_send,
+    piece_recv,
+    whole_send,
+    whole_recv,
+    up_send,
+    up_recv,
+):
+    seq_count, model_count = lax.axis_size("seq"), lax.axis_size("mp")
+    count = seq_count * model_count
+    seq, x = lax.axis_index("seq"), lax.axis_index("mp")
+    me = seq * model_count + x
+    rows = low_ref.shape[0] // count
+    size = up_ref.shape[2]
+    width = tokens_all.shape[1]
+    own = down_out.shape[0]
+    span = window.shape[1]
+    barrier = pltpu.get_barrier_semaphore()
+    first = jnp.minimum(me * own // 128, (width - span) // 128)
+    load = pltpu.make_async_copy(
+        tokens_all.at[:, pl.ds(pl.multiple_of(first * 128, 128), span)], window, window_sem
+    )
+    load.start()
+
+    def device(j):
+        to = lax.rem(me + j, count)
+        return to, (to // model_count, lax.rem(to, model_count))
+
+    def greet(j, carry):
+        pl.semaphore_signal(barrier, inc=1, device_id=device(j)[1], device_id_type=MESH)
+        return carry
+
+    lax.fori_loop(1, count, greet, 0)
+    pl.semaphore_wait(barrier, count - 1)
+
+    def at(block):
+        return pl.ds(pl.multiple_of(block * rows, rows), rows)
+
+    def piece_copy(j):
+        to, where = device(j)
+        return pltpu.make_async_remote_copy(
+            src_ref=low_ref.at[at(to), :],
+            dst_ref=pieces.at[j],
+            send_sem=piece_send.at[j],
+            recv_sem=piece_recv.at[j],
+            device_id=where,
+            device_id_type=MESH,
+        )
+
+    def whole_copy(j, block):
+        return pltpu.make_async_remote_copy(
+            src_ref=whole.at[at(block), :],
+            dst_ref=whole.at[at(block), :],
+            send_sem=whole_send.at[j],
+            recv_sem=whole_recv.at[j],
+            device_id=device(j)[1],
+            device_id_type=MESH,
+        )
+
+    def up_copy(j, block):
+        return pltpu.make_async_remote_copy(
+            src_ref=up_ref,
+            dst_ref=up_out.at[:, :, pl.ds(pl.multiple_of(block * size, size), size)],
+            send_sem=up_send.at[j],
+            recv_sem=up_recv.at[j],
+            device_id=(lax.rem(seq + j, seq_count), x),
+            device_id_type=MESH,
+        )
+
+    def loop(start, stop, act):
+        def body(j, carry):
+            act(j)
+            return carry
+
+        lax.fori_loop(start, stop, body, 0)
+
+    loop(1, count, lambda j: piece_copy(j).start())
+    loop(1, seq_count, lambda j: up_copy(j, seq).start())
+    up_out[:, :, pl.ds(pl.multiple_of(seq * size, size), size)] = up_ref[...]
+
+    def add(j, total):
+        piece_copy(j).wait_recv()
+        return total + pieces[j].astype(jnp.float32)
+
+    total = lax.fori_loop(1, count, add, low_ref[at(me), :].astype(jnp.float32))
+    whole[at(me), :] = total.astype(jnp.bfloat16)
+    loop(1, count, lambda j: whole_copy(j, me).start())
+    loop(1, count, lambda j: whole_copy(j, lax.rem(me - j + count, count)).wait_recv())
+    load.wait()
+    product[...] = dot_f32(window[...], whole[...], (0, 0))
+    down_out[...] = product[pl.ds(pl.multiple_of(me * own - first * 128, 8), own), :]
+    loop(1, count, lambda j: piece_copy(j).wait_send())
+    loop(1, count, lambda j: whole_copy(j, me).wait_send())
+    loop(1, seq_count, lambda j: up_copy(j, lax.rem(seq - j + seq_count, seq_count)).wait_recv())
+    loop(1, seq_count, lambda j: up_copy(j, seq).wait_send())
 
 
 def head_on_device(
@@ -280,26 +567,52 @@
     heads = decay_logarithms.shape[0]
     size = query_weight.shape[1] // heads
     rank = lifting_matrices.shape[1]
-    tokens_all = lax.all_gather(tokens, "seq", axis=0, tiled=True)
-    weights = jnp.stack([query_weight, key_weight, value_weight])
-    weights = lax.all_to_all(weights, "seq", split_axis=2, concat_axis=1, tiled=True)
-    upstream = lax.all_to_all(output_gradient, "seq", split_axis=1, concat_axis=0, tiled=True)
     cumulative = jnp.cumsum(decay_logarithms, axis=1)
-    cumulative = lax.all_to_all(cumulative, "seq", split_axis=0, concat_axis=1, tiled=True)
-    cumulative = cumulative.reshape(seq_count, length)
-    weight = jnp.concatenate([weights[0], weights[1], weights[2], adapter_down_maps], axis=1)
+    half = jnp.bfloat16
+    total_tokens = length * seq_count
+    anywhere = pl.BlockSpec(memory_space=pl.ANY)
+    in_vmem = pl.BlockSpec(memory_space=pltpu.VMEM)
+    dma = pltpu.SemaphoreType.DMA
+    layers = seq_count // 4
+    token_copies = (layers - 1) * 4 + 3 + layers * 2 + 2 * layers - 1
+    tokens_all, weight, upstream, cumulative = pl.pallas_call(
+        exchange_kernel,
+        out_shape=(
+            jax.ShapeDtypeStruct((total_tokens, width), half),
+            jax.ShapeDtypeStruct((width, 3 * size + 2 * rank), half),
+            jax.ShapeDtypeStruct((total_tokens, size), half),
+            jax.ShapeDtypeStruct((seq_count * heads, length), jnp.float32),
+        ),
+        in_specs=[anywhere] * 7,
+        out_specs=(anywhere,) * 4,
+        scratch_shapes=[
+            dma((7,)),
+            dma((token_copies,)),
+            dma((2 * seq_count,)),
+            dma((5, seq_count)),
+            dma((5, seq_count)),
+        ],
+        compiler_params=pltpu.CompilerParams(collective_id=0, has_side_effects=True),
+    )(
+        tokens,
+        query_weight,
+        key_weight,
+        value_weight,
+        adapter_down_maps,
+        output_gradient,
+        cumulative,
+    )
     lift = lax.dynamic_slice_in_dim(lifting_matrices, lax.axis_index("seq") * size, size, 2)
     lift = (adapter_scale * lift).astype(jnp.bfloat16)
     empty = jnp.zeros_like(lift[0])
     lift = jnp.concatenate(
         [jnp.concatenate([lift[0], empty], axis=1), jnp.concatenate([empty, lift[1]], axis=1)], axis=0
     )
-    total_tokens = length * seq_count
     low_gradient, up_products = pl.pallas_call(
         functools.partial(layer_kernel, rank),
         grid=(seq_count,),
         out_shape=(
-            jax.ShapeDtypeStruct((total_tokens, 2 * rank), jnp.float32),
+            jax.ShapeDtypeStruct((total_tokens, 2 * rank), half),
             jax.ShapeDtypeStruct((2, rank, size), jnp.float32),
         ),
         in_specs=[
@@ -324,22 +637,56 @@
             dimension_semantics=("arbitrary",), vmem_limit_bytes=48 * 1024 * 1024
         ),
     )(tokens_all, weight, lift, cumulative, upstream)
-    grad_up = lax.all_gather(up_products, "seq", axis=2, tiled=True)
-    whole_low = lax.psum(low_gradient, ("seq", "mp"))
+    count = seq_count * model_count
+    own_rows = width // count
+    span = 256
+    grad_down, grad_up = pl.pallas_call(
+        reduce_kernel,
+        out_shape=(
+            jax.ShapeDtypeStruct((own_rows, 2 * rank), jnp.float32),
+            jax.ShapeDtypeStruct((2, rank, size * seq_count), jnp.float32),
+        ),
+        in_specs=[in_vmem, in_vmem, anywhere],
+        out_specs=(in_vmem, in_vmem),
+        scratch_shapes=[
+            pltpu.VMEM((count, total_tokens // count, 2 * rank), half),
+            pltpu.VMEM((total_tokens, 2 * rank), half),
+            pltpu.VMEM((total_tokens, span), half),
+            pltpu.VMEM((span, 2 * rank), jnp.float32),
+            dma(()),
+            dma((count,)),
+            dma((count,)),
+            dma((count,)),
+            dma((count,)),
+            dma((seq_count,)),
+            dma((seq_count,)),
+        ],
+        compiler_params=pltpu.CompilerParams(
+            collective_id=1, has_side_effects=True, vmem_limit_bytes=32 * 1024 * 1024
+        ),
+    )(low_gradient, up_products, tokens_all)
+    return (grad_down, grad_up)
+
+
+def per_device(*arrays):
+    length, width = arrays[0].shape
+    heads = arrays[6].shape[0]
+    seq_count, model_count = lax.axis_size("seq"), lax.axis_size("mp")
+    size = arrays[1].shape[1] // heads
+    rank = arrays[5].shape[1]
     own_rows = width // (seq_count * model_count)
-    place = lax.axis_index("seq") * model_count + lax.axis_index("mp")
-    mine = lax.dynamic_slice_in_dim(tokens_all, place * own_rows, own_rows, 1)
-    grad_down = lax.dot_general(
-        mine, whole_low.astype(jnp.bfloat16), (((0,), (0,)), ((), ())), preferred_element_type=jnp.float32
-    )
-    return (grad_down, grad_up)
-
-
-def per_device(*arrays):
-    decay = arrays[6]
-    one_head = decay.shape[0] == lax.axis_size("seq")
-    square = decay.shape[1] == arrays[1].shape[1] // decay.shape[0]
-    return (head_on_device if one_head and square else on_device)(*arrays)
+    fits = (
+        heads == seq_count
+        and seq_count % 4 == 0
+        and model_count == 2
+        and length == size == 2 * rank == 128
+        and arrays[1].shape[0] % 16 == 0
+        and heads % 8 == 0
+        and own_rows % 8 == 0
+        and own_rows <= 128
+        and (length // model_count) % 16 == 0
+    )
+    return (head_on_device if fits else on_device)(*arrays)
 
 
 def solution(mesh):

time: 317 us -> 215 us (0.68)
  Pallas kernels: 27.9 us -> 198 us
  waiting for transfers between devices: 140 us -> 0 us
  starting transfers between devices: 53.3 us -> 0 us
  blocking collectives: 52.7 us -> 0 us
  between operations: 14.1 us -> 0.7 us
  local copies, waits for them, and re-layouts: 19.1 us -> 10.7 us
  other arithmetic: 6.43 us -> 2.35 us
    pallas_call x0 -> x2, Pallas kernels: none -> 171 us  [the longest x1 93.7 us: head_on_device(): pl.pallas_call(exchange_kernel, out_shape=(jax.ShapeDtypeStruct((total_to...]
    all_to_all x3 -> x0, waiting for transfers between devices: 139 us -> none  [the longest x1 136 us: head_on_device(): lax.all_to_all(weights, 'seq', split_axis=2, concat_axis=1, tiled=True)]
    all_to_all x3 -> x0, starting transfers between devices: 53.2 us -> none  [the longest x1 39.8 us: head_on_device(): lax.all_to_all(output_gradient, 'seq', split_axis=1, concat_axis=0, tiled...]
    psum x1 -> x0, blocking collectives: 52.7 us -> none  [head_on_device(): whole_low = lax.psum(low_gradient, ('seq', 'mp'))]
    all_to_all x2 -> x0, local copies, waits for them, and re-layouts: 7.95 us -> none  [the longest x1 7.02 us: head_on_device(): lax.all_to_all(weights, 'seq', split_axis=2, concat_axis=1, tiled=True)]
    unnamed x7 -> x10, local copies, waits for them, and re-layouts: 4.36 us -> 10.7 us
    another operation x1 -> x0, local copies, waits for them, and re-layouts: 4.76 us -> none  [head_on_device(): weights = jnp.stack([query_weight, key_weight, value_weight])]
  transfers between devices with their start and end apart: 5 -> 0, of which waited for: 2 -> 0; matrix products, arithmetic and copies ran while one was open for 7% -> 0% of each run, Pallas kernels for 0% -> 0%
where the time goes in v2:
time: 215 us; the launch traced here: 212 us
  Pallas kernels  198 us (92%)
  local copies, waits for them, and re-layouts  10.7 us (5%)
  other arithmetic  2.35 us (1%)
    pallas_call x1, Pallas kernels, head_on_device(): pl.pallas_call(exchange_kernel, out_shape=(jax.ShapeDtypeStruct((total_to...  93.7 us
    pallas_call x1, Pallas kernels, head_on_device(): pl.pallas_call(reduce_kernel, out_shape=(jax.ShapeDtypeStruct((own_rows,...  77.4 us
    pallas_call x1, Pallas kernels, head_on_device(): pl.pallas_call(functools.partial(layer_kernel, rank), grid=(seq_count,),...  27.3 us
    unnamed x10, local copies, waits for them, and re-layouts  10.7 us

profile of v2, /device:TPU:0, one launch (start us, length us, event | category | flops | bytes accessed | tf_op | source)
XLA Modules:
  0.0 212.1 jit_solution(17443569272277699825)
XLA Ops:
  0.6 1.6 reduce_window_sum.11.cumulative_ref
  2.2 0.8 dynamic-slice_multiply_fusion
  3.0 93.7 %shard_map.95 = (bf16[2048,3584]{1,0:T(8,128)(2,1)}, bf16[3584,512]{1,0:T(8,128)(2,1)}, bf16[2048,128]{1,0:T(8,128)(2,1)}, f32[256,128]{1,0:T(8,128)}) custom-call(bf16[128,3584]{1,0:T(8,128)(2,1)} %tokens_ref.1, bf16[224,2048]{1,0:T(8,128)(2,1)} %query_ref.1, bf16[224,2048]{1,0:T(8,128)(2,1)} %key_ref.1, bf16[224,2048]{1,0:T(8,128)(2,1)} %value_ref.1, ...), custom_call_target="tpu_custom_call" | custom-call | tf_op jit(solution)/shard_map/pallas_call | solution.py:578
  96.7 0.0 copy-start.1
  96.7 2.0 copy-done.1
  98.7 0.0 copy-start.2
  98.7 1.0 copy-done.2
  99.8 0.0 copy-start.3
  99.8 0.9 copy-done.3
  100.7 27.3 %shard_map.96 = (bf16[2048,128]{1,0:T(8,128)(2,1)S(1)}, f32[2,64,128]{2,1,0:T(8,128)S(1)}) custom-call(bf16[2048,3584]{1,0:T(8,128)(2,1)} %get-tuple-element.8.tokens_ref.tokens_all, bf16[3584,512]{1,0:T(8,128)(2,1)S(1)} %copy-done.1, bf16[128,256]{1,0:T(8,128)(2,1)S(1)} %fusion.2.lift_ref, f32[256,128]{1,0:T(8,128)S(1)} %copy-done.3, ...), custom_call_target="tpu_custom_call" | custom-call | tf_op jit(solution)/shard_map/pallas_call | solution.py:611
  128.0 0.0 copy-start
  128.0 5.2 %copy-done = bf16[2048,3584]{1,0:T(8,128)(2,1)S(1)} copy-done((bf16[2048,3584]{1,0:T(8,128)(2,1)S(1)}, bf16[2048,3584]{1,0:T(8,128)(2,1)}, u32[]{:S(2)}) %copy-start) | copy-done | bytes 14680088
  133.1 77.4 %shard_map.97 = (f32[112,128]{1,0:T(8,128)S(1)}, f32[2,64,2048]{2,1,0:T(8,128)S(1)}) custom-call(bf16[2048,128]{1,0:T(8,128)(2,1)S(1)} %get-tuple-element.12.low_ref, f32[2,64,128]{2,1,0:T(8,128)S(1)} %get-tuple-element.13.up_ref, bf16[2048,3584]{1,0:T(8,128)(2,1)S(1)} %copy-done), custom_call_target="tpu_custom_call" | custom-call | tf_op jit(solution)/shard_map/pallas_call | solution.py:643
  210.5 0.6 copy.12
  211.2 1.0 copy.13
  (2 shorter events, 0.0 us)
Async XLA Ops:
  96.7 2.0 copy-start.1
  98.7 1.0 copy-start.2
  99.8 0.9 copy-start.3
  128.0 5.2 %copy-start = (bf16[2048,3584]{1,0:T(8,128)(2,1)S(1)}, bf16[2048,3584]{1,0:T(8,128)(2,1)}, u32[]{:S(2)}) copy-start(bf16[2048,3584]{1,0:T(8,128)(2,1)} %get-tuple-element.8.tokens_ref.tokens_all) | copy-start | bytes 44040196

commit v3 on v2

--- a/solution.py
+++ b/solution.py
@@ -281,6 +281,7 @@
     upstream_all,
     cumulative_all,
     local_sem,
+    hop_send,
     token_send,
     token_recv,
     block_send,
@@ -376,8 +377,39 @@
             for k, (source_ref, dst_ref) in enumerate(pairs)
         ], pairs
 
-    for j in range(1, layers):
-        send(me, x, (seq_of(lax.rem(z + j, layers), y, core), x), own=True)
+    near = jnp.minimum(z, layers - 1 - z)
+
+    def layer_at(j):
+        side = jnp.where(2 * z < layers - 1, z + j - near, z - j + near)
+        pair = z - (j + 1) // 2 if j % 2 else z + j // 2
+        return z if j == 0 else jnp.where(j <= 2 * near, pair, side)
+
+    hops = []
+
+    def hop(block, up, own=False):
+        to = jnp.where(up, z + 1, z - 1)
+        inside = jnp.logical_and(to >= 0, to < layers)
+        index = len(hops)
+
+        def copy():
+            part = pl.ds(pl.multiple_of(x * half, half), half)
+            return pltpu.make_async_remote_copy(
+                src_ref=tokens_ref.at[part, :] if own else tokens_all.at[rows_of(block, x), :],
+                dst_ref=tokens_all.at[rows_of(block, x), :],
+                send_sem=hop_send.at[index],
+                recv_sem=token_recv.at[block * 2 + x],
+                device_id=(seq_of(to, y, core), x),
+                device_id_type=MESH,
+            )
+
+        hops.append((inside, copy))
+
+        @pl.when(inside)
+        def _():
+            copy().start()
+
+    hop(me, True, own=True)
+    hop(me, False, own=True)
     send(me, x, over_y, own=True)
     send(me, 0, sibling, own=True)
     send(me, 1, sibling, own=True)
@@ -398,14 +430,16 @@
         copy.start()
 
     def along_z(j):
-        block = seq_of(lax.rem(z - j + layers, layers), y, core)
+        layer = layer_at(j)
+        block = seq_of(layer, y, core)
         arrived(block, x)
+        hop(block, layer < z)
         send(block, x, over_y)
         send(block, x, over_x)
         send(block, x, sibling)
 
     def along_y(j):
-        block = seq_of(lax.rem(z - j + layers, layers), 1 - y, core)
+        block = seq_of(layer_at(j), 1 - y, core)
         arrived(block, x)
         send(block, x, over_x)
         send(block, x, sibling)
@@ -413,7 +447,7 @@
     def along_x(j):
         for other in range(2) if j else (1,):
             yy = 1 - y if other else y
-            block = seq_of(lax.rem(z - j + layers, layers), yy, core)
+            block = seq_of(layer_at(j), yy, core)
             arrived(block, 1 - x)
             send(block, 1 - x, sibling)
 
@@ -442,6 +476,11 @@
         copy.wait()
     for copy in sent:
         copy.wait_send()
+    for inside, copy in hops:
+
+        @pl.when(inside)
+        def _(copy=copy):
+            copy().wait_send()
 
 
 def reduce_kernel(
@@ -450,11 +489,14 @@
     tokens_all,
     down_out,
     up_out,
+    mate,
+    summed,
     pieces,
     whole,
     window,
     product,
     window_sem,
+    mate_sem,
     piece_send,
     piece_recv,
     whole_send,
@@ -462,15 +504,17 @@
     up_send,
     up_recv,
 ):
-    seq_count, model_count = lax.axis_size("seq"), lax.axis_size("mp")
-    count = seq_count * model_count
+    chips = lax.axis_size("seq") // 2
+    group = chips * 2
     seq, x = lax.axis_index("seq"), lax.axis_index("mp")
-    me = seq * model_count + x
-    rows = low_ref.shape[0] // count
+    chip, core = seq // 2, lax.rem(seq, 2)
+    me, place = seq * 2 + x, chip * 2 + x
+    rows = pieces.shape[1]
     size = up_ref.shape[2]
     width = tokens_all.shape[1]
     own = down_out.shape[0]
     span = window.shape[1]
+    sibling = (chip * 2 + 1 - core, x)
     barrier = pltpu.get_barrier_semaphore()
     first = jnp.minimum(me * own // 128, (width - span) // 128)
     load = pltpu.make_async_copy(
@@ -478,50 +522,13 @@
     )
     load.start()
 
+    def peer(j):
+        to = lax.rem(place + j, group)
+        return to // 2, lax.rem(to, 2)
+
     def device(j):
-        to = lax.rem(me + j, count)
-        return to, (to // model_count, lax.rem(to, model_count))
-
-    def greet(j, carry):
-        pl.semaphore_signal(barrier, inc=1, device_id=device(j)[1], device_id_type=MESH)
-        return carry
-
-    lax.fori_loop(1, count, greet, 0)
-    pl.semaphore_wait(barrier, count - 1)
-
-    def at(block):
-        return pl.ds(pl.multiple_of(block * rows, rows), rows)
-
-    def piece_copy(j):
-        to, where = device(j)
-        return pltpu.make_async_remote_copy(
-            src_ref=low_ref.at[at(to), :],
-            dst_ref=pieces.at[j],
-            send_sem=piece_send.at[j],
-            recv_sem=piece_recv.at[j],
-            device_id=where,
-            device_id_type=MESH,
-        )
-
-    def whole_copy(j, block):
-        return pltpu.make_async_remote_copy(
-            src_ref=whole.at[at(block), :],
-            dst_ref=whole.at[at(block), :],
-            send_sem=whole_send.at[j],
-            recv_sem=whole_recv.at[j],
-            device_id=device(j)[1],
-            device_id_type=MESH,
-        )
-
-    def up_copy(j, block):
-        return pltpu.make_async_remote_copy(
-            src_ref=up_ref,
-            dst_ref=up_out.at[:, :, pl.ds(pl.multiple_of(block * size, size), size)],
-            send_sem=up_send.at[j],
-            recv_sem=up_recv.at[j],
-            device_id=(lax.rem(seq + j, seq_count), x),
-            device_id_type=MESH,
-        )
+        to, to_x = peer(j)
+        return to * 2 + core, to_x
 
     def loop(start, stop, act):
         def body(j, carry):
@@ -530,25 +537,126 @@
 
         lax.fori_loop(start, stop, body, 0)
 
-    loop(1, count, lambda j: piece_copy(j).start())
-    loop(1, seq_count, lambda j: up_copy(j, seq).start())
+    def greet(where):
+        pl.semaphore_signal(barrier, inc=1, device_id=where, device_id_type=MESH)
+
+    greet(sibling)
+    loop(1, group, lambda j: greet(device(j)))
+    pl.semaphore_wait(barrier, group)
+
+    def remote(source, target, send_sem, recv_sem, where):
+        return pltpu.make_async_remote_copy(
+            src_ref=source,
+            dst_ref=target,
+            send_sem=send_sem,
+            recv_sem=recv_sem,
+            device_id=where,
+            device_id_type=MESH,
+        )
+
+    def landed(at, sem):
+        pltpu.make_async_copy(at, at, sem).wait()
+
+    swap = remote(low_ref.at[:, 1 - core], mate, mate_sem.at[0], mate_sem.at[1], sibling)
+    swap.start()
+
+    def up_at(block):
+        return up_out.at[:, :, pl.ds(pl.multiple_of(block * size, size), size)]
+
+    def up_copy(j):
+        where = (lax.rem(chip + j, chips) * 2 + core, x)
+        return remote(up_ref, up_at(seq), up_send.at[j], up_recv.at[seq], where)
+
+    def up_forward(j):
+        block = lax.rem(chip - j + chips, chips) * 2 + core
+        return remote(
+            up_at(block), up_at(block), up_send.at[chips + j], up_recv.at[block], sibling
+        )
+
+    up_own = remote(up_ref, up_at(seq), up_send.at[chips], up_recv.at[seq], sibling)
+
+    def piece_copy(j):
+        to, to_x = peer(j)
+        part = summed.at[to, pl.ds(pl.multiple_of(to_x * rows, rows), rows), :]
+        return remote(part, pieces.at[j], piece_send.at[j], piece_recv.at[j], device(j))
+
+    def whole_at(block):
+        return whole.at[pl.ds(pl.multiple_of(block * rows, rows), rows), :]
+
+    def whole_copy(j):
+        return remote(whole_at(me), whole_at(me), whole_send.at[j], whole_recv.at[me], device(j))
+
+    def from_peer(j):
+        where = device(group - j)
+        return where[0] * 2 + where[1]
+
+    def whole_forward(j):
+        at = whole_at(from_peer(j))
+        return remote(at, at, whole_send.at[group + j], whole_recv.at[from_peer(j)], sibling)
+
+    swap.wait_recv()
+    summed[...] = (low_ref[:, core].astype(jnp.float32) + mate[...].astype(jnp.float32)).astype(
+        summed.dtype
+    )
+    loop(1, group, lambda j: piece_copy(j).start())
+    up_own.start()
+    loop(1, chips, lambda j: up_copy(j).start())
     up_out[:, :, pl.ds(pl.multiple_of(seq * size, size), size)] = up_ref[...]
 
     def add(j, total):
-        piece_copy(j).wait_recv()
+        landed(pieces.at[j], piece_recv.at[j])
         return total + pieces[j].astype(jnp.float32)
 
-    total = lax.fori_loop(1, count, add, low_ref[at(me), :].astype(jnp.float32))
-    whole[at(me), :] = total.astype(jnp.bfloat16)
-    loop(1, count, lambda j: whole_copy(j, me).start())
-    loop(1, count, lambda j: whole_copy(j, lax.rem(me - j + count, count)).wait_recv())
+    mine = summed[chip, pl.ds(pl.multiple_of(x * rows, rows), rows), :].astype(jnp.float32)
+    total = lax.fori_loop(1, group, add, mine)
+    whole[pl.ds(pl.multiple_of(me * rows, rows), rows), :] = total.astype(whole.dtype)
+    whole_own = remote(
+        whole_at(me), whole_at(me), whole_send.at[group], whole_recv.at[me], sibling
+    )
+    loop(1, group, lambda j: whole_copy(j).start())
+    whole_own.start()
+
+    def pass_up(j):
+        block = lax.rem(chip - j + chips, chips) * 2 + core
+        landed(up_at(block), up_recv.at[block])
+        up_forward(j).start()
+
+    def pass_whole(j):
+        landed(whole_at(from_peer(j)), whole_recv.at[from_peer(j)])
+        whole_forward(j).start()
+
+    loop(1, group, pass_whole)
+    loop(1, chips, pass_up)
+
+    def from_sibling(j):
+        block = (j // 2 * 2 + 1 - core) * 2 + lax.rem(j, 2)
+        landed(whole_at(block), whole_recv.at[block])
+
+    loop(0, group, from_sibling)
     load.wait()
     product[...] = dot_f32(window[...], whole[...], (0, 0))
     down_out[...] = product[pl.ds(pl.multiple_of(me * own - first * 128, 8), own), :]
-    loop(1, count, lambda j: piece_copy(j).wait_send())
-    loop(1, count, lambda j: whole_copy(j, me).wait_send())
-    loop(1, seq_count, lambda j: up_copy(j, lax.rem(seq - j + seq_count, seq_count)).wait_recv())
-    loop(1, seq_count, lambda j: up_copy(j, seq).wait_send())
+
+    def up_sibling(j):
+        block = j * 2 + 1 - core
+        landed(up_at(block), up_recv.at[block])
+
+    loop(0, chips, up_sibling)
+    swap.wait_send()
+    up_own.wait_send()
+    whole_own.wait_send()
+
+    def sends(j):
+        piece_copy(j).wait_send()
+        whole_copy(j).wait_send()
+        whole_forward(j).wait_send()
+
+    def up_sends(j):
+        up_copy(j).wait_send()
+        up_forward(j).wait_send()
+
+    loop(1, group, sends)
+    loop(1, chips, up_sends)
 
 
 def head_on_device(
@@ -574,7 +682,7 @@
     in_vmem = pl.BlockSpec(memory_space=pltpu.VMEM)
     dma = pltpu.SemaphoreType.DMA
     layers = seq_count // 4
-    token_copies = (layers - 1) * 4 + 3 + layers * 2 + 2 * layers - 1
+    token_copies = (layers - 1) * 3 + 3 + layers * 2 + 2 * layers - 1
     tokens_all, weight, upstream, cumulative = pl.pallas_call(
         exchange_kernel,
         out_shape=(
@@ -587,6 +695,7 @@
         out_specs=(anywhere,) * 4,
         scratch_shapes=[
             dma((7,)),
+            dma((layers + 1,)),
             dma((token_copies,)),
             dma((2 * seq_count,)),
             dma((5, seq_count)),
@@ -649,22 +758,27 @@
         in_specs=[in_vmem, in_vmem, anywhere],
         out_specs=(in_vmem, in_vmem),
         scratch_shapes=[
-            pltpu.VMEM((count, total_tokens // count, 2 * rank), half),
+            pltpu.VMEM((seq_count // 2, length, 2 * rank), half),
+            pltpu.VMEM((seq_count // 2, length, 2 * rank), half),
+            pltpu.VMEM((seq_count, length // 2, 2 * rank), half),
             pltpu.VMEM((total_tokens, 2 * rank), half),
             pltpu.VMEM((total_tokens, span), half),
             pltpu.VMEM((span, 2 * rank), jnp.float32),
             dma(()),
-            dma((count,)),
-            dma((count,)),
+            dma((2,)),
+            dma((seq_count,)),
+            dma((seq_count,)),
             dma((count,)),
             dma((count,)),
             dma((seq_count,)),
             dma((seq_count,)),
         ],
         compiler_params=pltpu.CompilerParams(
-            collective_id=1, has_side_effects=True, vmem_limit_bytes=32 * 1024 * 1024
+            collective_id=1, has_side_effects=True, vmem_limit_bytes=56 * 1024 * 1024
         ),
-    )(low_gradient, up_products, tokens_all)
+    )(
+        low_gradient.reshape(seq_count // 2, 2, length, 2 * rank), up_products, tokens_all
+    )
     return (grad_down, grad_up)
 
 

time: 215 us -> 220 us (1.023); the launches traced: 212 us -> 219 us
  Pallas kernels: 198 us -> 207 us
    pallas_call x1, Pallas kernels: 93.7 us -> 147 us  [head_on_device(): pl.pallas_call(exchange_kernel, out_shape=(jax.ShapeDtypeStruct((total_to...]
    pallas_call x1, Pallas kernels: 77.4 us -> 32.8 us  [head_on_device(): pl.pallas_call(reduce_kernel, out_shape=(jax.ShapeDtypeStruct((own_rows,...]
    unnamed x10 -> x12, local copies, waits for them, and re-layouts: 10.7 us -> 9.13 us
where the time goes in v3:
time: 220 us; the launch traced here: 219 us
  Pallas kernels  207 us (94%)
  local copies, waits for them, and re-layouts  9.13 us (4%)
  other arithmetic  2.35 us (1%)
    pallas_call x1, Pallas kernels, head_on_device(): pl.pallas_call(exchange_kernel, out_shape=(jax.ShapeDtypeStruct((total_to...  147 us
    pallas_call x1, Pallas kernels, head_on_device(): pl.pallas_call(reduce_kernel, out_shape=(jax.ShapeDtypeStruct((own_rows,...  32.8 us
    pallas_call x1, Pallas kernels, head_on_device(): pl.pallas_call(functools.partial(layer_kernel, rank), grid=(seq_count,),...  27.2 us
    unnamed x12, local copies, waits for them, and re-layouts  9.13 us

profile of v3, /device:TPU:0, one launch (start us, length us, event | category | flops | bytes accessed | tf_op | source)
XLA Modules:
  0.0 219.4 jit_solution(6122176001283585167)
XLA Ops:
  0.6 1.6 reduce_window_sum.11.cumulative_ref
  2.2 0.8 dynamic-slice_multiply_fusion
  3.0 147.2 %shard_map.95 = (bf16[2048,3584]{1,0:T(8,128)(2,1)}, bf16[3584,512]{1,0:T(8,128)(2,1)}, bf16[2048,128]{1,0:T(8,128)(2,1)}, f32[256,128]{1,0:T(8,128)}) custom-call(bf16[128,3584]{1,0:T(8,128)(2,1)} %tokens_ref.1, bf16[224,2048]{1,0:T(8,128)(2,1)} %query_ref.1, bf16[224,2048]{1,0:T(8,128)(2,1)} %key_ref.1, bf16[224,2048]{1,0:T(8,128)(2,1)} %value_ref.1, ...), custom_call_target="tpu_custom_call" | custom-call | tf_op jit(solution)/shard_map/pallas_call | solution.py:686
  150.2 0.0 copy-start
  150.2 2.0 copy-done
  152.2 0.0 copy-start.1
  152.2 1.0 copy-done.1
  153.3 0.0 copy-start.3
  153.3 0.9 copy-done.3
  154.2 27.2 %shard_map.96 = (bf16[2048,128]{1,0:T(8,128)(2,1)S(1)}, f32[2,64,128]{2,1,0:T(8,128)S(1)}) custom-call(bf16[2048,3584]{1,0:T(8,128)(2,1)} %get-tuple-element.8.tokens_ref.tokens_all, bf16[3584,512]{1,0:T(8,128)(2,1)S(1)} %copy-done, bf16[128,256]{1,0:T(8,128)(2,1)S(1)} %fusion.2.lift_ref, f32[256,128]{1,0:T(8,128)S(1)} %copy-done.3, ...), custom_call_target="tpu_custom_call" | custom-call | tf_op jit(solution)/shard_map/pallas_call | solution.py:720
  181.4 0.0 copy-start.2
  181.4 0.8 copy-done.2
  182.2 0.0 copy-start.4
  182.2 0.6 copy-done.4
  182.8 32.8 %shard_map.97 = (f32[112,128]{1,0:T(8,128)}, f32[2,64,2048]{2,1,0:T(8,128)}) custom-call(bf16[8,2,128,128]{3,2,1,0:T(8,128)(2,1)} %bitcast.5, f32[2,64,128]{2,1,0:T(8,128)} %copy-done.4, bf16[2048,3584]{1,0:T(8,128)(2,1)} %get-tuple-element.8.tokens_ref.tokens_all), custom_call_target="tpu_custom_call" | custom-call | tf_op jit(solution)/shard_map/pallas_call | solution.py:752
  215.6 1.4 copy.12
  217.1 2.3 %copy.13 = f32[2,64,2048]{2,1,0:T(8,128)} copy(f32[2,64,2048]{2,1,0:T(8,128)} %get-tuple-element.19) | data formatting | bytes 2097152
  (2 shorter events, 0.0 us)
Async XLA Ops:
  150.2 2.0 copy-start
  152.2 1.0 copy-start.1
  153.3 0.9 copy-start.3
  181.4 0.8 copy-start.2
  182.2 0.6 copy-start.4

commit v4 on v3

--- a/solution.py
+++ b/solution.py
@@ -281,7 +281,6 @@
     upstream_all,
     cumulative_all,
     local_sem,
-    hop_send,
     token_send,
     token_recv,
     block_send,
@@ -377,39 +376,8 @@
             for k, (source_ref, dst_ref) in enumerate(pairs)
         ], pairs
 
-    near = jnp.minimum(z, layers - 1 - z)
-
-    def layer_at(j):
-        side = jnp.where(2 * z < layers - 1, z + j - near, z - j + near)
-        pair = z - (j + 1) // 2 if j % 2 else z + j // 2
-        return z if j == 0 else jnp.where(j <= 2 * near, pair, side)
-
-    hops = []
-
-    def hop(block, up, own=False):
-        to = jnp.where(up, z + 1, z - 1)
-        inside = jnp.logical_and(to >= 0, to < layers)
-        index = len(hops)
-
-        def copy():
-            part = pl.ds(pl.multiple_of(x * half, half), half)
-            return pltpu.make_async_remote_copy(
-                src_ref=tokens_ref.at[part, :] if own else tokens_all.at[rows_of(block, x), :],
-                dst_ref=tokens_all.at[rows_of(block, x), :],
-                send_sem=hop_send.at[index],
-                recv_sem=token_recv.at[block * 2 + x],
-                device_id=(seq_of(to, y, core), x),
-                device_id_type=MESH,
-            )
-
-        hops.append((inside, copy))
-
-        @pl.when(inside)
-        def _():
-            copy().start()
-
-    hop(me, True, own=True)
-    hop(me, False, own=True)
+    for j in range(1, layers):
+        send(me, x, (seq_of(lax.rem(z + j, layers), y, core), x), own=True)
     send(me, x, over_y, own=True)
     send(me, 0, sibling, own=True)
     send(me, 1, sibling, own=True)
@@ -430,16 +398,14 @@
         copy.start()
 
     def along_z(j):
-        layer = layer_at(j)
-        block = seq_of(layer, y, core)
+        block = seq_of(lax.rem(z - j + layers, layers), y, core)
         arrived(block, x)
-        hop(block, layer < z)
         send(block, x, over_y)
         send(block, x, over_x)
         send(block, x, sibling)
 
     def along_y(j):
-        block = seq_of(layer_at(j), 1 - y, core)
+        block = seq_of(lax.rem(z - j + layers, layers), 1 - y, core)
         arrived(block, x)
         send(block, x, over_x)
         send(block, x, sibling)
@@ -447,7 +413,7 @@
     def along_x(j):
         for other in range(2) if j else (1,):
             yy = 1 - y if other else y
-            block = seq_of(layer_at(j), yy, core)
+            block = seq_of(lax.rem(z - j + layers, layers), yy, core)
             arrived(block, 1 - x)
             send(block, 1 - x, sibling)
 
@@ -476,11 +442,6 @@
         copy.wait()
     for copy in sent:
         copy.wait_send()
-    for inside, copy in hops:
-
-        @pl.when(inside)
-        def _(copy=copy):
-            copy().wait_send()
 
 
 def reduce_kernel(
@@ -682,7 +643,7 @@
     in_vmem = pl.BlockSpec(memory_space=pltpu.VMEM)
     dma = pltpu.SemaphoreType.DMA
     layers = seq_count // 4
-    token_copies = (layers - 1) * 3 + 3 + layers * 2 + 2 * layers - 1
+    token_copies = (layers - 1) * 4 + 3 + layers * 2 + 2 * layers - 1
     tokens_all, weight, upstream, cumulative = pl.pallas_call(
         exchange_kernel,
         out_shape=(
@@ -695,7 +656,6 @@
         out_specs=(anywhere,) * 4,
         scratch_shapes=[
             dma((7,)),
-            dma((layers + 1,)),
             dma((token_copies,)),
             dma((2 * seq_count,)),
             dma((5, seq_count)),

time: 220 us -> 194 us (0.88)
  Pallas kernels: 207 us -> 181 us
    pallas_call x1, Pallas kernels: 147 us -> 93.7 us  [head_on_device(): pl.pallas_call(exchange_kernel, out_shape=(jax.ShapeDtypeStruct((total_to...]
    pallas_call x1, Pallas kernels: 32.8 us -> 60.4 us  [head_on_device(): pl.pallas_call(reduce_kernel, out_shape=(jax.ShapeDtypeStruct((own_rows,...]
where the time goes in v4:
time: 194 us
  Pallas kernels  181 us (93%)
  local copies, waits for them, and re-layouts  9.13 us (5%)
  other arithmetic  2.35 us (1%)
    pallas_call x1, Pallas kernels, head_on_device(): pl.pallas_call(exchange_kernel, out_shape=(jax.ShapeDtypeStruct((total_to...  93.7 us
    pallas_call x1, Pallas kernels, head_on_device(): pl.pallas_call(reduce_kernel, out_shape=(jax.ShapeDtypeStruct((own_rows,...  60.4 us
    pallas_call x1, Pallas kernels, head_on_device(): pl.pallas_call(functools.partial(layer_kernel, rank), grid=(seq_count,),...  27.3 us
    unnamed x12, local copies, waits for them, and re-layouts  9.13 us

profile of v4, /device:TPU:0, one launch (start us, length us, event | category | flops | bytes accessed | tf_op | source)
XLA Modules:
  0.0 193.6 jit_solution(2130632691121844738)
XLA Ops:
  0.6 1.6 reduce_window_sum.11.cumulative_ref
  2.2 0.8 dynamic-slice_multiply_fusion
  3.0 93.7 %shard_map.95 = (bf16[2048,3584]{1,0:T(8,128)(2,1)}, bf16[3584,512]{1,0:T(8,128)(2,1)}, bf16[2048,128]{1,0:T(8,128)(2,1)}, f32[256,128]{1,0:T(8,128)}) custom-call(bf16[128,3584]{1,0:T(8,128)(2,1)} %tokens_ref.1, bf16[224,2048]{1,0:T(8,128)(2,1)} %query_ref.1, bf16[224,2048]{1,0:T(8,128)(2,1)} %key_ref.1, bf16[224,2048]{1,0:T(8,128)(2,1)} %value_ref.1, ...), custom_call_target="tpu_custom_call" | custom-call | tf_op jit(solution)/shard_map/pallas_call | solution.py:647
  96.7 0.0 copy-start
  96.7 2.0 %copy-done = bf16[3584,512]{1,0:T(8,128)(2,1)S(1)} copy-done((bf16[3584,512]{1,0:T(8,128)(2,1)S(1)}, bf16[3584,512]{1,0:T(8,128)(2,1)}, u32[]{:S(2)}) %copy-start) | copy-done | bytes 3670040
  98.7 0.0 copy-start.1
  98.7 1.0 copy-done.1
  99.8 0.0 copy-start.3
  99.8 0.9 copy-done.3
  100.7 27.3 %shard_map.96 = (bf16[2048,128]{1,0:T(8,128)(2,1)S(1)}, f32[2,64,128]{2,1,0:T(8,128)S(1)}) custom-call(bf16[2048,3584]{1,0:T(8,128)(2,1)} %get-tuple-element.8.tokens_ref.tokens_all, bf16[3584,512]{1,0:T(8,128)(2,1)S(1)} %copy-done, bf16[128,256]{1,0:T(8,128)(2,1)S(1)} %fusion.2.lift_ref, f32[256,128]{1,0:T(8,128)S(1)} %copy-done.3, ...), custom_call_target="tpu_custom_call" | custom-call | tf_op jit(solution)/shard_map/pallas_call | solution.py:680
  128.0 0.0 copy-start.2
  128.0 0.8 copy-done.2
  128.8 0.0 copy-start.4
  128.8 0.6 copy-done.4
  129.4 60.4 %shard_map.97 = (f32[112,128]{1,0:T(8,128)}, f32[2,64,2048]{2,1,0:T(8,128)}) custom-call(bf16[8,2,128,128]{3,2,1,0:T(8,128)(2,1)} %bitcast.5, f32[2,64,128]{2,1,0:T(8,128)} %copy-done.4, bf16[2048,3584]{1,0:T(8,128)(2,1)} %get-tuple-element.8.tokens_ref.tokens_all), custom_call_target="tpu_custom_call" | custom-call | tf_op jit(solution)/shard_map/pallas_call | solution.py:712
  189.8 1.4 copy.12
  191.3 2.3 %copy.13 = f32[2,64,2048]{2,1,0:T(8,128)} copy(f32[2,64,2048]{2,1,0:T(8,128)} %get-tuple-element.19) | data formatting | bytes 2097152
  (2 shorter events, 0.0 us)
Async XLA Ops:
  96.7 2.0 %copy-start = (bf16[3584,512]{1,0:T(8,128)(2,1)S(1)}, bf16[3584,512]{1,0:T(8,128)(2,1)}, u32[]{:S(2)}) copy-start(bf16[3584,512]{1,0:T(8,128)(2,1)} %get-tuple-element.9.weight_ref) | copy-start | bytes 11010052
  98.7 1.0 copy-start.1
  99.8 0.9 copy-start.3
  128.0 0.8 copy-start.2
  128.8 0.6 copy-start.4
